TPU v7x, 32 devices: a whole 2x2x4 slice. The times are simulated.
32 devices in a mesh: gx: 4 (over z), gy: 8 (over y, x, core).
Axes of the slice: x: 2, y: 2, z: 4, core: 2. Of those that a mesh axis runs over, the one named last changes fastest.
Arguments:
- speed_factor: float32 [64, 128, 256], P('gx', 'gy'), may hold values from 0.05 to 0.17
- wave_before: float32 [64, 128, 256], P('gx', 'gy'), may hold values from -6 to 6
- wave_now: float32 [64, 128, 256], P('gx', 'gy'), may hold values from -6 to 6
- source_accel: float32 [2, 64, 128, 256], P(None, 'gx', 'gy'), may hold values from -4 to 4
- prior_image: float32 [64, 128, 256], P('gx', 'gy'), may hold values from -40 to 40
- conv_first: bfloat16 [27, 1, 8], replicated, may hold values from -1.25 to 1.25
- bias_first: float32 [8], replicated, may hold values from -3 to 3
- conv_middle: bfloat16 [27, 8, 8], replicated, may hold values from -0.4375 to 0.4375
- bias_middle: float32 [8], replicated, may hold values from -3 to 3
- conv_last: bfloat16 [27, 8, 1], replicated, may hold values from -0.4375 to 0.4375
Outputs:
- wave_next: float32 [64, 128, 256], P('gx', 'gy')
- wave_after: float32 [64, 128, 256], P('gx', 'gy')
- gradient: float32 [64, 128, 256], P('gx', 'gy')
- model_step: float32 [64, 128, 256], P('gx', 'gy')
All inputs are finite; a program needn't handle non-finite values.
Results may differ from a plain program's by a relative error of at most 0.0059.
Values may be sent and summed in bfloat16 or wider, within the bound.
A program may use at most 192 MiB of HBM per device.

v0:
```python
import functools

import jax
import jax.numpy as jnp
from jax import lax
from jax.experimental import pallas as pl
from jax.experimental.pallas import tpu as pltpu
from jax.sharding import PartitionSpec as P

COEFS = (-205.0 / 72.0, 8.0 / 5.0, -1.0 / 5.0, 8.0 / 315.0, -1.0 / 560.0)
MESH = pl.DeviceIdType.MESH
F32 = jnp.float32
BF16 = jnp.bfloat16


def shift_z(v, k):
    depth = v.shape[-1]
    lane = lax.broadcasted_iota(jnp.int32, v.shape, v.ndim - 1)
    rolled = pltpu.roll(v, (-k) % depth, v.ndim - 1)
    return jnp.where((lane + k >= 0) & (lane + k < depth), rolled, 0.0)


def laplace_plane(ext, x, ny):
    center = ext[x + 4, 8 : 8 + ny, :]
    total = 3.0 * COEFS[0] * center
    for k in range(1, 5):
        cycle = ext[x + 4 + k, 8 : 8 + ny, :] + ext[x + 4 - k, 8 : 8 + ny, :]
        cycle = cycle + ext[x + 4, 8 + k : 8 + k + ny, :]
        cycle = cycle + ext[x + 4, 8 - k : 8 - k + ny, :]
        cycle = cycle + shift_z(center, k) + shift_z(center, -k)
        total = total + COEFS[k] * cycle
    return center, total


def kernel(
    n_gx,
    n_gy,
    speed,
    before,
    now,
    src,
    prior,
    s1,
    s2,
    s3,
    b1,
    b2,
    out_next,
    out_after,
    out_grad,
    out_step,
    ext_a,
    ext_b,
    pack_a,
    pack_b,
    recv_a,
    recv_b,
    grad,
    pack_g,
    recv_g,
    h1,
    h2,
    w1,
    w2,
    w3,
    part,
    red_y,
    red_x,
    send_sem,
    recv_sem,
    ry_send,
    ry_recv,
    rx_send,
    rx_recv,
):
    nx, ny, depth = now.shape
    gx, gy = lax.axis_index("gx"), lax.axis_index("gy")
    barrier = pltpu.get_barrier_semaphore()

    def there(dx, dy):
        ok = None
        for pos, d, n in ((gx, dx, n_gx), (gy, dy, n_gy)):
            if d:
                one = (pos + d >= 0) & (pos + d < n)
                ok = one if ok is None else ok & one
        return ok

    for i in range(1, n_gy):
        pl.semaphore_signal(
            barrier, inc=1, device_id=(gx, lax.rem(gy + i, n_gy)), device_id_type=MESH
        )
    for i in range(1, n_gx):
        pl.semaphore_signal(
            barrier, inc=1, device_id=(lax.rem(gx + i, n_gx), gy), device_id_type=MESH
        )
    diagonals = ((-1, -1), (-1, 1), (1, -1), (1, 1))
    for dx, dy in diagonals:

        @pl.when(there(dx, dy))
        def _(dx=dx, dy=dy):
            pl.semaphore_signal(barrier, inc=1, device_id=(gx + dx, gy + dy), device_id_type=MESH)

    class Copy:
        def __init__(self, ident, source, target, dx, dy):
            self.make = lambda: pltpu.make_async_remote_copy(
                src_ref=source,
                dst_ref=target,
                send_sem=send_sem.at[ident],
                recv_sem=recv_sem.at[ident],
                device_id=(gx + dx, gy + dy),
                device_id_type=MESH,
            )
            self.to = there(dx, dy)
            self.origin = there(-dx, -dy)
            self.target = target

        def start(self):
            @pl.when(self.to)
            def _():
                self.make().start()

        def clear(self):
            @pl.when(jnp.logical_not(self.origin))
            def _():
                self.target[...] = jnp.zeros(self.target.shape, self.target.dtype)

        def arrive(self):
            @pl.when(self.origin)
            def _():
                self.make().wait_recv()

        def sent(self):
            @pl.when(self.to)
            def _():
                self.make().wait_send()

    own = pl.ds(8, ny)

    def wave_copies(base, ext, pack, recv):
        return (
            Copy(base, ext.at[pl.ds(nx, 4), own, :], ext.at[pl.ds(0, 4), own, :], 1, 0),
            Copy(base + 1, ext.at[pl.ds(4, 4), own, :], ext.at[pl.ds(nx + 4, 4), own, :], -1, 0),
            Copy(base + 2, pack.at[1], recv.at[0], 0, 1),
            Copy(base + 3, pack.at[0], recv.at[1], 0, -1),
        )

    copies_a = wave_copies(0, ext_a, pack_a, recv_a)
    copies_b = wave_copies(4, ext_b, pack_b, recv_b)
    row16 = pl.ds(0, ny)
    groups = nx // 4
    mid = pl.ds(1, groups)
    copies_g = (
        Copy(8, grad.at[pl.ds(nx, 4), row16, :], grad.at[pl.ds(0, 4), row16, :], 1, 0),
        Copy(9, grad.at[pl.ds(4, 4), row16, :], grad.at[pl.ds(nx + 4, 4), row16, :], -1, 0),
        Copy(10, pack_g.at[1], recv_g.at[0, mid], 0, 1),
        Copy(11, pack_g.at[0], recv_g.at[1, mid], 0, -1),
        Copy(12, pack_g.at[1, groups - 1], recv_g.at[0, 0], 1, 1),
        Copy(13, pack_g.at[1, 0], recv_g.at[0, groups + 1], -1, 1),
        Copy(14, pack_g.at[0, groups - 1], recv_g.at[1, 0], 1, -1),
        Copy(15, pack_g.at[0, 0], recv_g.at[1, groups + 1], -1, -1),
    )

    def pack_wave(ext, pack):
        half = nx // 2
        for i in range(half):
            for side, at in ((0, 8), (1, 8 + ny - 4)):
                pack[side, i] = jnp.concatenate(
                    [ext[4 + i, at : at + 4, :], ext[4 + half + i, at : at + 4, :]], axis=0
                )

    def unpack_wave(ext, recv):
        half = nx // 2
        for i in range(half):
            for side, at in ((0, 4), (1, 8 + ny)):
                tile = recv[side, i]
                ext[4 + i, at : at + 4, :] = tile[0:4]
                ext[4 + half + i, at : at + 4, :] = tile[4:8]

    ext_a[pl.ds(4, nx), own, :] = now[...]
    pack_wave(ext_a, pack_a)
    for group in (copies_a, copies_b, copies_g):
        for c in group:
            c.clear()

    wanted = (n_gy - 1) + (n_gx - 1)
    for dx, dy in diagonals:
        wanted = wanted + there(dx, dy).astype(jnp.int32)
    pl.semaphore_wait(barrier, wanted)
    for c in copies_a:
        c.start()

    def band(out, slabs, e, rows, per_row, first_out, width, place):
        shape = (rows * per_row, 3 * width)
        col = lax.broadcasted_iota(jnp.int32, shape, 1)
        row = lax.broadcasted_iota(jnp.int32, shape, 0)
        slot = col - jnp.where(col >= width, width, 0) - jnp.where(col >= 2 * width, width, 0)
        y_out = (row >> 3 if per_row == 8 else row) + first_out
        gap = place(slot) - y_out
        total = jnp.zeros(shape, F32)
        for b in range(3):
            slab = slabs[3 * b + e]
            if per_row == 8:
                full = jnp.concatenate([slab] * rows, axis=0)
            else:
                full = jnp.broadcast_to(slab, shape)
            total = jnp.where(gap == b - 1, full, total)
        out[e * shape[0] : (e + 1) * shape[0], :] = total.astype(BF16)

    def grad_slot(slot):
        return jnp.where(
            slot < ny, slot, jnp.where(slot < ny + 4, slot - ny - 4, jnp.where(slot < ny + 8, slot - 4, 999))
        )

    r1, r2 = ny + 4, ny + 2
    for e in range(3):
        band(w1, s1, e, r1, 8, -2, 2 * ny, grad_slot)
        band(w2, s2, e, r2, 8, -1, r1 * 8, lambda s: (s >> 3) - 2)
        band(w3, s3, e, ny, 1, 0, r2 * 8, lambda s: (s >> 3) - 1)

    for c in copies_a:
        c.arrive()
    unpack_wave(ext_a, recv_a)

    def step_one(x, carry):
        center, lap = laplace_plane(ext_a, x, ny)
        value = 2.0 * center - before[x] + speed[x] * lap
        out_next[x] = value
        ext_b[x + 4, 8 : 8 + ny, :] = value
        return carry

    lax.fori_loop(0, nx, step_one, 0)
    pack_wave(ext_b, pack_b)
    for c in copies_b:
        c.start()
    for c in copies_b:
        c.arrive()
    unpack_wave(ext_b, recv_b)

    def step_two(x, carry):
        center, lap = laplace_plane(ext_b, x, ny)
        value = 2.0 * center - now[x] + speed[x] * lap
        out_after[x] = value
        gradient = prior[x] + src[0, x] * center + src[1, x] * value
        out_grad[x] = gradient
        grad[x + 4, 0:ny, :] = gradient.astype(BF16)
        return carry

    lax.fori_loop(0, nx, step_two, 0)
    for t in range(groups):
        for side, at in ((0, 0), (1, ny - 4)):
            pack_g[side, t] = jnp.concatenate(
                [out_grad[4 * t + j, at : at + 4, :] for j in range(4)], axis=0
            ).astype(BF16)
    for c in copies_g:
        c.start()
    for c in copies_g:
        c.arrive()
    for t in range(groups + 2):
        low = recv_g[0, t].astype(F32)
        high = recv_g[1, t].astype(F32)
        for j in range(4):
            grad[4 * t + j, ny : 2 * ny, :] = jnp.concatenate(
                [low[4 * j : 4 * j + 4], high[4 * j : 4 * j + 4], jnp.zeros((ny - 8, depth), F32)],
                axis=0,
            ).astype(BF16)

    x_min = jnp.where(gx == 0, 0, -8)
    x_max = jnp.where(gx == n_gx - 1, nx, nx + 8)
    y_min = jnp.where(gy == 0, 0, -8)
    y_max = jnp.where(gy == n_gy - 1, ny, ny + 8)

    def conv_plane(weight, rhs, rows):
        res = jnp.dot(weight[...], rhs, preferred_element_type=F32)
        return (
            res[rows : 2 * rows] + shift_z(res[:rows], -1) + shift_z(res[2 * rows :], 1)
        )

    def hidden(value, bias, rows, first, x):
        y = (lax.broadcasted_iota(jnp.int32, value.shape, 0) >> 3) + first
        inside = (y >= y_min) & (y < y_max) & (x >= x_min) & (x < x_max)
        full = jnp.concatenate([jnp.broadcast_to(bias[...], (8, depth))] * rows, axis=0)
        return jnp.where(inside, jnp.maximum(value + full, 0.0), 0.0).astype(BF16)

    m1, m2 = 8 * r1, 8 * r2

    def layer_one(p, carry):
        rhs = grad[pl.ds(p + 1, 3)].reshape(6 * ny, depth)
        h1[p] = hidden(conv_plane(w1, rhs, m1), b1, r1, -2, p - 2)
        return carry

    lax.fori_loop(0, nx + 4, layer_one, 0)

    def layer_two(p, carry):
        rhs = h1[pl.ds(p, 3)].reshape(3 * m1, depth)
        h2[p] = hidden(conv_plane(w2, rhs, m2), b2, r2, -1, p - 1)
        return carry

    lax.fori_loop(0, nx + 2, layer_two, 0)

    zero = jnp.zeros((ny, depth), F32)

    def layer_three(p, carry):
        gg, gd, dd = carry
        rhs = h2[pl.ds(p, 3)].reshape(3 * m2, depth)
        g = out_grad[p]
        d = conv_plane(w3, rhs, ny) + g
        out_step[p] = d
        return gg + g * g, gd + g * d, dd + d * d

    sums = lax.fori_loop(0, nx, layer_three, (zero, zero, zero))
    row = lax.broadcasted_iota(jnp.int32, (8, depth), 0)
    tile = jnp.zeros((8, depth), F32)
    for i, s in enumerate(sums):
        tile = jnp.where(row == i, jnp.sum(s, axis=0, keepdims=True), tile)
    folded = tile[:, 0:128]
    for i in range(1, depth // 128):
        folded = folded + tile[:, 128 * i : 128 * i + 128]

    def reduce_over(value, slot, slots, me, n, sends, recvs, peer_id):
        part[slot] = value
        slots[me] = value
        todo = []
        for i in range(1, n):
            c = pltpu.make_async_remote_copy(
                src_ref=part.at[slot],
                dst_ref=slots.at[me],
                send_sem=sends.at[i],
                recv_sem=recvs.at[i],
                device_id=peer_id(lax.rem(me + i, n)),
                device_id_type=MESH,
            )
            c.start()
            todo.append(c)
        for i, c in enumerate(todo):
            back = pltpu.make_async_remote_copy(
                src_ref=part.at[slot],
                dst_ref=slots.at[lax.rem(me + n - (i + 1), n)],
                send_sem=sends.at[i + 1],
                recv_sem=recvs.at[i + 1],
                device_id=peer_id(lax.rem(me + i + 1, n)),
                device_id_type=MESH,
            )
            back.wait_recv()
        total = slots[0]
        for i in range(1, n):
            total = total + slots[i]
        return total, todo

    over_y, todo_y = reduce_over(folded, 0, red_y, gy, n_gy, ry_send, ry_recv, lambda j: (gx, j))
    total, todo_x = reduce_over(over_y, 1, red_x, gx, n_gx, rx_send, rx_recv, lambda j: (j, gy))
    sums = jnp.sum(total, axis=1, keepdims=True)
    damping = 8.0 * float(nx * n_gx * ny * n_gy * depth)
    scale = sums[1:2] / (sums[0:1] + sums[2:3] + damping)

    def finish(p, carry):
        out_step[p] = scale * out_step[p]
        return carry

    lax.fori_loop(0, nx, finish, 0)
    for group in (copies_a, copies_b, copies_g):
        for c in group:
            c.sent()
    for c in todo_y + todo_x:
        c.wait_send()


def slabs(weight, slots):
    _, c, d = weight.shape
    w = weight.astype(F32).reshape(3, 9, c, d).transpose(1, 3, 0, 2)
    w = jnp.broadcast_to(w[:, :, :, None, :], (9, d, 3, slots, c))
    return w.reshape(9, d, 3 * slots * c)


def shards(n_gx, n_gy, speed, before, now, src, prior, w_first, b_first, w_mid, b_mid, w_last):
    nx, ny, depth = now.shape
    out = jax.ShapeDtypeStruct(now.shape, F32)
    vmem = pl.BlockSpec(memory_space=pltpu.VMEM)
    half, groups = nx // 2, nx // 4
    r1, r2 = ny + 4, ny + 2
    ch = b_first.shape[0]
    return pl.pallas_call(
        functools.partial(kernel, n_gx, n_gy),
        out_shape=(out,) * 4,
        in_specs=[vmem] * 10,
        out_specs=(vmem,) * 4,
        scratch_shapes=[
            pltpu.VMEM((nx + 8, ny + 16, depth), F32),
            pltpu.VMEM((nx + 8, ny + 16, depth), F32),
            pltpu.VMEM((2, half, 8, depth), F32),
            pltpu.VMEM((2, half, 8, depth), F32),
            pltpu.VMEM((2, half, 8, depth), F32),
            pltpu.VMEM((2, half, 8, depth), F32),
            pltpu.VMEM((nx + 8, 2 * ny, depth), BF16),
            pltpu.VMEM((2, groups, 16, depth), BF16),
            pltpu.VMEM((2, groups + 2, 16, depth), BF16),
            pltpu.VMEM((nx + 4, r1 * ch, depth), BF16),
            pltpu.VMEM((nx + 2, r2 * ch, depth), BF16),
            pltpu.VMEM((3 * r1 * ch, 6 * ny), BF16),
            pltpu.VMEM((3 * r2 * ch, 3 * r1 * ch), BF16),
            pltpu.VMEM((3 * ny, 3 * r2 * ch), BF16),
            pltpu.VMEM((2, 8, 128), F32),
            pltpu.VMEM((n_gy, 8, 128), F32),
            pltpu.VMEM((n_gx, 8, 128), F32),
            pltpu.SemaphoreType.DMA((16,)),
            pltpu.SemaphoreType.DMA((16,)),
            pltpu.SemaphoreType.DMA((n_gy,)),
            pltpu.SemaphoreType.DMA((n_gy,)),
            pltpu.SemaphoreType.DMA((n_gx,)),
            pltpu.SemaphoreType.DMA((n_gx,)),
        ],
        compiler_params=pltpu.CompilerParams(
            collective_id=0, has_side_effects=True, vmem_limit_bytes=40 * 1024 * 1024
        ),
    )(
        speed,
        before,
        now,
        src,
        prior,
        slabs(w_first, 2 * ny),
        slabs(w_mid, r1),
        slabs(w_last, r2),
        b_first.reshape(ch, 1),
        b_mid.reshape(ch, 1),
    )


def solution(mesh):
    brick = P("gx", "gy", None)
    return jax.shard_map(
        functools.partial(shards, mesh.shape["gx"], mesh.shape["gy"]),
        mesh=mesh,
        in_specs=(brick, brick, brick, P(None, "gx", "gy", None), brick, P(), P(), P(), P(), P()),
        out_specs=(brick,) * 4,
        check_vma=False,
    )
```

profile of v0, /device:TPU:0, one launch (start us, length us, event | category | flops | bytes accessed | tf_op | source)
XLA Modules:
  0.0 55.1 jit_solution(13378151997516570321)
XLA Ops:
  0.6 0.8 %reshape.52 = f32[3,9,8,8]{1,0,3,2:T(4,128)S(1)} reshape(bf16[27,8,8]{0,2,1:T(8,128)(2,1)} %param.17) | data formatting | bytes 10368 | tf_op jit(solution)/shard_map/transpose | solution.py:369
  1.5 0.3 copy.20
  1.8 0.0 copy-start.5
  1.8 0.0 copy-start.6
  1.8 1.7 %broadcast_in_dim.34 = f32[9,8,3,20,8]{4,3,2,1,0:T(8,128)} broadcast(f32[9,8,3,8]{3,2,1,0:T(4,128)S(1)} %copy.20), dimensions={0,1,2,4} | broadcast | bytes 145152 | tf_op jit(solution)/shard_map/broadcast_in_dim | solution.py:370
  3.5 0.0 copy-start.7
  3.5 0.0 copy-start.8
  3.5 0.0 copy-start
  3.5 0.0 copy-start.1
  3.5 0.0 copy-start.2
  3.5 0.0 copy-start.3
  3.5 0.0 copy-start.4
  3.5 2.4 %reshape.46.s2 = f32[9,8,480]{2,1,0:T(8,128)S(1)} reshape(f32[9,8,3,20,8]{4,3,2,1,0:T(8,128)} %broadcast_in_dim.34) | data formatting | bytes 276480 | tf_op jit(solution)/shard_map/reshape | solution.py:371
  6.0 0.0 copy-done.5
  6.0 0.1 reshape.54
  6.1 0.1 copy.21
  6.2 0.2 broadcast_in_dim.45.s3
  6.4 0.0 copy-done.6
  6.4 0.1 reshape.53
  6.5 0.1 copy.19
  6.6 0.1 broadcast_in_dim.32
  6.7 0.1 broadcast_in_dim.33.s1
  6.9 0.0 copy-done.7
  6.9 0.1 copy.23.b1
  7.0 0.0 copy-done.8
  7.0 0.1 copy.24.b2
  7.0 0.0 copy-done
  7.0 0.0 copy-done.1
  7.0 0.0 copy-done.2
  7.0 0.0 copy-done.3
  7.1 0.0 copy-done.4
  7.1 45.2 %shard_map.129 = (f32[16,16,256]{2,1,0:T(8,128)S(1)}, f32[16,16,256]{2,1,0:T(8,128)S(1)}, f32[16,16,256]{2,1,0:T(8,128)S(1)}, f32[16,16,256]{2,1,0:T(8,128)S(1)}) custom-call(f32[16,16,256]{2,1,0:T(8,128)S(1)} %copy-done.1, f32[16,16,256]{2,1,0:T(8,128)S(1)} %copy-done.2, f32[16,16,256]{2,1,0:T(8,128)S(1)} %copy-done.3, f32[2,16,16,256]{3,2,1,0:T(8,128)S(1)} %copy-done, ...), custom_call_target="tpu_custom_call" | custom-call | tf_op jit(solution)/shard_map/pallas_call | solution.py:381
  52.2 0.7 %copy.29 = f32[16,16,256]{2,1,0:T(8,128)} copy(f32[16,16,256]{2,1,0:T(8,128)S(1)} %get-tuple-element.8) | data formatting | bytes 524288
  52.9 0.7 %copy.30 = f32[16,16,256]{2,1,0:T(8,128)} copy(f32[16,16,256]{2,1,0:T(8,128)S(1)} %get-tuple-element.9) | data formatting | bytes 524288
  53.6 0.7 %copy.31 = f32[16,16,256]{2,1,0:T(8,128)} copy(f32[16,16,256]{2,1,0:T(8,128)S(1)} %get-tuple-element.10) | data formatting | bytes 524288
  54.4 0.7 %copy.32 = f32[16,16,256]{2,1,0:T(8,128)} copy(f32[16,16,256]{2,1,0:T(8,128)S(1)} %get-tuple-element.11) | data formatting | bytes 524288
  (1 shorter events, 0.0 us)
Async XLA Ops:
  1.8 4.2 %copy-start.5 = (bf16[27,8,1]{0,1,2:T(8,128)(2,1)S(1)}, bf16[27,8,1]{0,1,2:T(8,128)(2,1)}, u32[]{:S(2)}) copy-start(bf16[27,8,1]{0,1,2:T(8,128)(2,1)} %param.19) | copy-start | bytes 1300
  1.8 4.6 %copy-start.6 = (bf16[27,1,8]{0,2,1:T(8,128)(2,1)S(1)}, bf16[27,1,8]{0,2,1:T(8,128)(2,1)}, u32[]{:S(2)}) copy-start(bf16[27,1,8]{0,2,1:T(8,128)(2,1)} %param.15) | copy-start | bytes 1300
  3.5 3.4 %copy-start.7 = (f32[8]{0:T(128)S(1)}, f32[8]{0:T(128)}, u32[]{:S(2)}) copy-start(f32[8]{0:T(128)} %param.16) | copy-start | bytes 100
  3.5 3.5 %copy-start.8 = (f32[8]{0:T(128)S(1)}, f32[8]{0:T(128)}, u32[]{:S(2)}) copy-start(f32[8]{0:T(128)} %param.18) | copy-start | bytes 100
  3.5 3.6 %copy-start = (f32[2,16,16,256]{3,2,1,0:T(8,128)S(1)}, f32[2,16,16,256]{3,2,1,0:T(8,128)}, u32[]{:S(2)}) copy-start(f32[2,16,16,256]{3,2,1,0:T(8,128)} %src.1) | copy-start | bytes 1572868
  3.5 3.6 %copy-start.1 = (f32[16,16,256]{2,1,0:T(8,128)S(1)}, f32[16,16,256]{2,1,0:T(8,128)}, u32[]{:S(2)}) copy-start(f32[16,16,256]{2,1,0:T(8,128)} %speed.1) | copy-start | bytes 786436
  3.5 3.6 %copy-start.2 = (f32[16,16,256]{2,1,0:T(8,128)S(1)}, f32[16,16,256]{2,1,0:T(8,128)}, u32[]{:S(2)}) copy-start(f32[16,16,256]{2,1,0:T(8,128)} %before.1) | copy-start | bytes 786436
  3.5 3.5 %copy-start.3 = (f32[16,16,256]{2,1,0:T(8,128)S(1)}, f32[16,16,256]{2,1,0:T(8,128)}, u32[]{:S(2)}) copy-start(f32[16,16,256]{2,1,0:T(8,128)} %now.1) | copy-start | bytes 786436
  3.5 3.5 %copy-start.4 = (f32[16,16,256]{2,1,0:T(8,128)S(1)}, f32[16,16,256]{2,1,0:T(8,128)}, u32[]{:S(2)}) copy-start(f32[16,16,256]{2,1,0:T(8,128)} %prior.1) | copy-start | bytes 786436
where the time goes:
time: 55.3 us; the launch traced here: 55.1 us
  Pallas kernels  45.2 us (82%)
  local copies, waits for them, and re-layouts  9.13 us (17%)
  between operations  0.76 us (1%)
    pallas_call x1, Pallas kernels, shards(): pl.pallas_call(functools.partial(kernel, n_gx, n_gy), out_shape=(out,) *...  45.2 us
    unnamed x22, local copies, waits for them, and re-layouts  2.85 us
    broadcast_in_dim x9, local copies, waits for them, and re-layouts, slabs(): w = jnp.broadcast_to(w[:, :, :, None, :], (9, d, 3, slots, c))  2.56 us
    reshape x1, local copies, waits for them, and re-layouts, slabs(): return w.reshape(9, d, 3 * slots * c)  2.43 us
    transpose x2, local copies, waits for them, and re-layouts, slabs(): w = weight.astype(F32).reshape(3, 9, c, d).transpose(1, 3, 0, 2)  1.12 us

commit v1 on v0

--- a/solution.py
+++ b/solution.py
@@ -11,6 +11,8 @@
 MESH = pl.DeviceIdType.MESH
 F32 = jnp.float32
 BF16 = jnp.bfloat16
+UNROLL = True
+WAVE_UNROLL = 4
 
 
 def shift_z(v, k):
@@ -212,9 +214,17 @@
         )
 
     r1, r2 = ny + 4, ny + 2
+    m1, m2 = 8 * r1, 8 * r2
+    wide = 3 * m1
+    col = lax.broadcasted_iota(jnp.int32, (24, wide), 1)
+    row = lax.broadcasted_iota(jnp.int32, (24, wide), 0)
+    col_a = jnp.where(col >= m1, 1, 0) + jnp.where(col >= 2 * m1, 1, 0)
+    pick = jnp.where(row == 8 * col_a + (col & 7), 1.0, 0.0).astype(BF16)
+    s2_wide = jnp.dot(s2[...], pick, preferred_element_type=F32)
+    s2_slabs = [s2_wide[8 * k : 8 * k + 8] for k in range(9)]
     for e in range(3):
         band(w1, s1, e, r1, 8, -2, 2 * ny, grad_slot)
-        band(w2, s2, e, r2, 8, -1, r1 * 8, lambda s: (s >> 3) - 2)
+        band(w2, s2_slabs, e, r2, 8, -1, r1 * 8, lambda s: (s >> 3) - 2)
         band(w3, s3, e, ny, 1, 0, r2 * 8, lambda s: (s >> 3) - 1)
 
     for c in copies_a:
@@ -228,7 +238,7 @@
         ext_b[x + 4, 8 : 8 + ny, :] = value
         return carry
 
-    lax.fori_loop(0, nx, step_one, 0)
+    lax.fori_loop(0, nx, step_one, 0, unroll=WAVE_UNROLL)
     pack_wave(ext_b, pack_b)
     for c in copies_b:
         c.start()
@@ -245,7 +255,7 @@
         grad[x + 4, 0:ny, :] = gradient.astype(BF16)
         return carry
 
-    lax.fori_loop(0, nx, step_two, 0)
+    lax.fori_loop(0, nx, step_two, 0, unroll=WAVE_UNROLL)
     for t in range(groups):
         for side, at in ((0, 0), (1, ny - 4)):
             pack_g[side, t] = jnp.concatenate(
@@ -281,21 +291,19 @@
         full = jnp.concatenate([jnp.broadcast_to(bias[...], (8, depth))] * rows, axis=0)
         return jnp.where(inside, jnp.maximum(value + full, 0.0), 0.0).astype(BF16)
 
-    m1, m2 = 8 * r1, 8 * r2
-
     def layer_one(p, carry):
         rhs = grad[pl.ds(p + 1, 3)].reshape(6 * ny, depth)
         h1[p] = hidden(conv_plane(w1, rhs, m1), b1, r1, -2, p - 2)
         return carry
 
-    lax.fori_loop(0, nx + 4, layer_one, 0)
+    lax.fori_loop(0, nx + 4, layer_one, 0, unroll=UNROLL)
 
     def layer_two(p, carry):
         rhs = h1[pl.ds(p, 3)].reshape(3 * m1, depth)
         h2[p] = hidden(conv_plane(w2, rhs, m2), b2, r2, -1, p - 1)
         return carry
 
-    lax.fori_loop(0, nx + 2, layer_two, 0)
+    lax.fori_loop(0, nx + 2, layer_two, 0, unroll=UNROLL)
 
     zero = jnp.zeros((ny, depth), F32)
 
@@ -307,7 +315,7 @@
         out_step[p] = d
         return gg + g * g, gd + g * d, dd + d * d
 
-    sums = lax.fori_loop(0, nx, layer_three, (zero, zero, zero))
+    sums = lax.fori_loop(0, nx, layer_three, (zero, zero, zero), unroll=UNROLL)
     row = lax.broadcasted_iota(jnp.int32, (8, depth), 0)
     tile = jnp.zeros((8, depth), F32)
     for i, s in enumerate(sums):
@@ -356,7 +364,7 @@
         out_step[p] = scale * out_step[p]
         return carry
 
-    lax.fori_loop(0, nx, finish, 0)
+    lax.fori_loop(0, nx, finish, 0, unroll=4)
     for group in (copies_a, copies_b, copies_g):
         for c in group:
             c.sent()
@@ -418,7 +426,7 @@
         src,
         prior,
         slabs(w_first, 2 * ny),
-        slabs(w_mid, r1),
+        w_mid.reshape(3, 9, ch, ch).transpose(1, 3, 0, 2).reshape(9 * ch, 3 * ch),
         slabs(w_last, r2),
         b_first.reshape(ch, 1),
         b_mid.reshape(ch, 1),

time: 55.3 us -> 39.4 us (0.71)
  Pallas kernels: 45.2 us -> 29.2 us
    pallas_call x1, Pallas kernels: 45.2 us -> 29.2 us  [shards(): pl.pallas_call(functools.partial(kernel, n_gx, n_gy), out_shape=(out,) *...]
    unnamed x22 -> x24, local copies, waits for them, and re-layouts: 2.85 us -> 7.64 us
    reshape x1 -> x2, local copies, waits for them, and re-layouts: 2.43 us -> 0.19 us  [shards(): w_mid.reshape(3, 9, ch, ch).transpose(1, 3, 0, 2).reshape(9 * ch, 3 * ch)]
    broadcast_in_dim x9 -> x8, local copies, waits for them, and re-layouts: 2.56 us -> 0.83 us  [slabs(): w = jnp.broadcast_to(w[:, :, :, None, :], (9, d, 3, slots, c))]
    transpose x2 -> x1, local copies, waits for them, and re-layouts: 1.12 us -> 0.31 us  [shards(): w_mid.reshape(3, 9, ch, ch).transpose(1, 3, 0, 2).reshape(9 * ch, 3 * ch)]
where the time goes in v1:
time: 39.4 us; the launch traced here: 39.1 us
  Pallas kernels  29.2 us (74%)
  local copies, waits for them, and re-layouts  9.13 us (23%)
  between operations  0.74 us (2%)
    pallas_call x1, Pallas kernels, shards(): pl.pallas_call(functools.partial(kernel, n_gx, n_gy), out_shape=(out,) *...  29.2 us
    unnamed x24, local copies, waits for them, and re-layouts  7.64 us
    broadcast_in_dim x8, local copies, waits for them, and re-layouts, slabs(): w = jnp.broadcast_to(w[:, :, :, None, :], (9, d, 3, slots, c))  0.83 us

profile of v1, /device:TPU:0, one launch (start us, length us, event | category | flops | bytes accessed | tf_op | source)
XLA Modules:
  0.0 39.1 jit_solution(14457696281525599385)
XLA Ops:
  0.6 0.0 copy-start.8
  0.6 0.6 %copy-done.8 = f32[8]{0:T(128)S(1)} copy-done((f32[8]{0:T(128)S(1)}, f32[8]{0:T(128)}, u32[]{:S(2)}) %copy-start.8) | copy-done | bytes 56
  1.3 0.0 copy-start.9
  1.3 0.1 copy.23.b1
  1.4 0.6 %copy-done.9 = f32[8]{0:T(128)S(1)} copy-done((f32[8]{0:T(128)S(1)}, f32[8]{0:T(128)}, u32[]{:S(2)}) %copy-start.9) | copy-done | bytes 56
  1.9 0.0 copy-start.6
  1.9 0.1 copy.24.b2
  2.0 0.6 %copy-done.6 = bf16[27,1,8]{0,2,1:T(8,128)(2,1)S(1)} copy-done((bf16[27,1,8]{0,2,1:T(8,128)(2,1)S(1)}, bf16[27,1,8]{0,2,1:T(8,128)(2,1)}, u32[]{:S(2)}) %copy-start.6) | copy-done | bytes 456
  2.6 0.0 copy-start.7
  2.6 0.1 reshape.50
  2.7 0.6 %copy-done.7 = bf16[27,8,1]{0,1,2:T(8,128)(2,1)S(1)} copy-done((bf16[27,8,1]{0,1,2:T(8,128)(2,1)S(1)}, bf16[27,8,1]{0,1,2:T(8,128)(2,1)}, u32[]{:S(2)}) %copy-start.7) | copy-done | bytes 456
  3.3 0.1 reshape.51
  3.4 0.1 copy.21
  3.5 0.0 copy-start.5
  3.5 0.1 copy.19
  3.6 0.6 %copy-done.5 = bf16[27,8,8]{0,2,1:T(8,128)(2,1)S(1)} copy-done((bf16[27,8,8]{0,2,1:T(8,128)(2,1)S(1)}, bf16[27,8,8]{0,2,1:T(8,128)(2,1)}, u32[]{:S(2)}) %copy-start.5) | copy-done | bytes 3480
  4.2 0.0 copy-start.3
  4.2 0.1 reshape.43
  4.3 0.3 copy.20
  4.6 0.1 reshape.44.s2
  4.7 0.0 copy-start
  4.7 0.1 broadcast_in_dim.26
  4.9 0.1 broadcast_in_dim.27.s1
  5.0 0.0 copy-start.2
  5.0 0.0 copy-start.1
  5.1 0.2 broadcast_in_dim.38.s3
  5.2 0.0 copy-done.3
  5.2 0.6 %copy-done = f32[2,16,16,256]{3,2,1,0:T(8,128)S(1)} copy-done((f32[2,16,16,256]{3,2,1,0:T(8,128)S(1)}, f32[2,16,16,256]{3,2,1,0:T(8,128)}, u32[]{:S(2)}) %copy-start) | copy-done | bytes 524312
  5.8 0.2 copy-done.2
  6.0 0.1 copy-done.1
  6.1 0.0 copy-start.4
  6.1 0.9 %copy-done.4 = f32[16,16,256]{2,1,0:T(8,128)S(1)} copy-done((f32[16,16,256]{2,1,0:T(8,128)S(1)}, f32[16,16,256]{2,1,0:T(8,128)}, u32[]{:S(2)}) %copy-start.4) | copy-done | bytes 262168
  7.0 29.2 %shard_map.129 = (f32[16,16,256]{2,1,0:T(8,128)S(1)}, f32[16,16,256]{2,1,0:T(8,128)S(1)}, f32[16,16,256]{2,1,0:T(8,128)S(1)}, f32[16,16,256]{2,1,0:T(8,128)S(1)}) custom-call(f32[16,16,256]{2,1,0:T(8,128)S(1)} %copy-done.1, f32[16,16,256]{2,1,0:T(8,128)S(1)} %copy-done.2, f32[16,16,256]{2,1,0:T(8,128)S(1)} %copy-done.3, f32[2,16,16,256]{3,2,1,0:T(8,128)S(1)} %copy-done, ...), custom_call_target="tpu_custom_call" | custom-call | tf_op jit(solution)/shard_map/pallas_call | solution.py:389
  36.3 0.7 %copy.29 = f32[16,16,256]{2,1,0:T(8,128)} copy(f32[16,16,256]{2,1,0:T(8,128)S(1)} %get-tuple-element.8) | data formatting | bytes 524288
  37.0 0.7 %copy.30 = f32[16,16,256]{2,1,0:T(8,128)} copy(f32[16,16,256]{2,1,0:T(8,128)S(1)} %get-tuple-element.9) | data formatting | bytes 524288
  37.7 0.7 %copy.31 = f32[16,16,256]{2,1,0:T(8,128)} copy(f32[16,16,256]{2,1,0:T(8,128)S(1)} %get-tuple-element.10) | data formatting | bytes 524288
  38.4 0.7 %copy.32 = f32[16,16,256]{2,1,0:T(8,128)} copy(f32[16,16,256]{2,1,0:T(8,128)S(1)} %get-tuple-element.11) | data formatting | bytes 524288
  (1 shorter events, 0.0 us)
Async XLA Ops:
  0.6 0.7 %copy-start.8 = (f32[8]{0:T(128)S(1)}, f32[8]{0:T(128)}, u32[]{:S(2)}) copy-start(f32[8]{0:T(128)} %param.16) | copy-start | bytes 100
  1.3 0.7 %copy-start.9 = (f32[8]{0:T(128)S(1)}, f32[8]{0:T(128)}, u32[]{:S(2)}) copy-start(f32[8]{0:T(128)} %param.18) | copy-start | bytes 100
  1.9 0.7 %copy-start.6 = (bf16[27,1,8]{0,2,1:T(8,128)(2,1)S(1)}, bf16[27,1,8]{0,2,1:T(8,128)(2,1)}, u32[]{:S(2)}) copy-start(bf16[27,1,8]{0,2,1:T(8,128)(2,1)} %param.15) | copy-start | bytes 1300
  2.6 0.7 %copy-start.7 = (bf16[27,8,1]{0,1,2:T(8,128)(2,1)S(1)}, bf16[27,8,1]{0,1,2:T(8,128)(2,1)}, u32[]{:S(2)}) copy-start(bf16[27,8,1]{0,1,2:T(8,128)(2,1)} %param.19) | copy-start | bytes 1300
  3.5 0.7 %copy-start.5 = (bf16[27,8,8]{0,2,1:T(8,128)(2,1)S(1)}, bf16[27,8,8]{0,2,1:T(8,128)(2,1)}, u32[]{:S(2)}) copy-start(bf16[27,8,8]{0,2,1:T(8,128)(2,1)} %param.17) | copy-start | bytes 10372
  4.2 1.0 %copy-start.3 = (f32[16,16,256]{2,1,0:T(8,128)S(1)}, f32[16,16,256]{2,1,0:T(8,128)}, u32[]{:S(2)}) copy-start(f32[16,16,256]{2,1,0:T(8,128)} %now.1) | copy-start | bytes 786436
  4.7 1.1 %copy-start = (f32[2,16,16,256]{3,2,1,0:T(8,128)S(1)}, f32[2,16,16,256]{3,2,1,0:T(8,128)}, u32[]{:S(2)}) copy-start(f32[2,16,16,256]{3,2,1,0:T(8,128)} %src.1) | copy-start | bytes 1572868
  5.0 1.0 %copy-start.2 = (f32[16,16,256]{2,1,0:T(8,128)S(1)}, f32[16,16,256]{2,1,0:T(8,128)}, u32[]{:S(2)}) copy-start(f32[16,16,256]{2,1,0:T(8,128)} %before.1) | copy-start | bytes 786436
  5.0 1.0 %copy-start.1 = (f32[16,16,256]{2,1,0:T(8,128)S(1)}, f32[16,16,256]{2,1,0:T(8,128)}, u32[]{:S(2)}) copy-start(f32[16,16,256]{2,1,0:T(8,128)} %speed.1) | copy-start | bytes 786436
  6.1 0.9 %copy-start.4 = (f32[16,16,256]{2,1,0:T(8,128)S(1)}, f32[16,16,256]{2,1,0:T(8,128)}, u32[]{:S(2)}) copy-start(f32[16,16,256]{2,1,0:T(8,128)} %prior.1) | copy-start | bytes 786436

commit v2 on v1

--- a/solution.py
+++ b/solution.py
@@ -22,35 +22,43 @@
     return jnp.where((lane + k >= 0) & (lane + k < depth), rolled, 0.0)
 
 
-def laplace_plane(ext, x, ny):
-    center = ext[x + 4, 8 : 8 + ny, :]
+def laplace_z(center):
     total = 3.0 * COEFS[0] * center
+    for k in range(1, 5):
+        total = total + COEFS[k] * (shift_z(center, k) + shift_z(center, -k))
+    return total
+
+
+def laplace_xy(ext, x, ny):
+    total = None
     for k in range(1, 5):
         cycle = ext[x + 4 + k, 8 : 8 + ny, :] + ext[x + 4 - k, 8 : 8 + ny, :]
         cycle = cycle + ext[x + 4, 8 + k : 8 + k + ny, :]
         cycle = cycle + ext[x + 4, 8 - k : 8 - k + ny, :]
-        cycle = cycle + shift_z(center, k) + shift_z(center, -k)
-        total = total + COEFS[k] * cycle
-    return center, total
+        total = COEFS[k] * cycle if total is None else total + COEFS[k] * cycle
+    return total
 
 
 def kernel(
     n_gx,
     n_gy,
-    speed,
-    before,
-    now,
-    src,
-    prior,
-    s1,
-    s2,
-    s3,
-    b1,
-    b2,
+    speed_hbm,
+    before_hbm,
+    now_hbm,
+    src_hbm,
+    prior_hbm,
+    raw,
+    raw_b1,
+    raw_b2,
     out_next,
     out_after,
     out_grad,
     out_step,
+    speed,
+    before,
+    src,
+    prior,
+    load_sem,
     ext_a,
     ext_b,
     pack_a,
@@ -75,9 +83,24 @@
     rx_send,
     rx_recv,
 ):
-    nx, ny, depth = now.shape
+    nx, ny, depth = now_hbm.shape
     gx, gy = lax.axis_index("gx"), lax.axis_index("gy")
     barrier = pltpu.get_barrier_semaphore()
+    own = pl.ds(8, ny)
+    loads = [
+        pltpu.make_async_copy(source, target, load_sem.at[i])
+        for i, (source, target) in enumerate(
+            (
+                (now_hbm, ext_a.at[pl.ds(4, nx), own, :]),
+                (before_hbm, before),
+                (speed_hbm, speed),
+                (src_hbm, src),
+                (prior_hbm, prior),
+            )
+        )
+    ]
+    for load in loads:
+        load.start()
 
     def there(dx, dy):
         ok = None
@@ -135,8 +158,6 @@
             @pl.when(self.to)
             def _():
                 self.make().wait_send()
-
-    own = pl.ds(8, ny)
 
     def wave_copies(base, ext, pack, recv):
         return (
@@ -178,7 +199,7 @@
                 ext[4 + i, at : at + 4, :] = tile[0:4]
                 ext[4 + half + i, at : at + 4, :] = tile[4:8]
 
-    ext_a[pl.ds(4, nx), own, :] = now[...]
+    loads[0].wait()
     pack_wave(ext_a, pack_a)
     for group in (copies_a, copies_b, copies_g):
         for c in group:
@@ -215,25 +236,79 @@
 
     r1, r2 = ny + 4, ny + 2
     m1, m2 = 8 * r1, 8 * r2
-    wide = 3 * m1
-    col = lax.broadcasted_iota(jnp.int32, (24, wide), 1)
-    row = lax.broadcasted_iota(jnp.int32, (24, wide), 0)
-    col_a = jnp.where(col >= m1, 1, 0) + jnp.where(col >= 2 * m1, 1, 0)
-    pick = jnp.where(row == 8 * col_a + (col & 7), 1.0, 0.0).astype(BF16)
-    s2_wide = jnp.dot(s2[...], pick, preferred_element_type=F32)
-    s2_slabs = [s2_wide[8 * k : 8 * k + 8] for k in range(9)]
+    def third(index, size):
+        return jnp.where(index >= size, 1, 0) + jnp.where(index >= 2 * size, 1, 0)
+
+    def iota(shape, dim):
+        return lax.broadcasted_iota(jnp.int32, shape, dim)
+
+    def turned(rows):
+        eye = jnp.where(iota((8, 8), 0) == iota((8, 8), 1), 1.0, 0.0).astype(BF16)
+        return lax.dot_general(
+            eye, rows.astype(BF16), (((1,), (1,)), ((), ())), preferred_element_type=F32
+        )
+
+    def stacked(flat, step):
+        tall = jnp.concatenate([flat] * 9, axis=0)
+        tap = iota(tall.shape, 1) >> step
+        return jnp.where(tap - 9 * third(tap, 9) == iota(tall.shape, 0) >> 3, tall, 0.0).astype(BF16)
+
+    def matches(count, step, width):
+        shape = (count, 3 * width)
+        tap, col = iota(shape, 0), iota(shape, 1)
+        hit = third(tap >> step, 9) == third(col, width)
+        return hit & ((tap & 7) == (col & 7)) if step else hit
+
+    def one_hot(hit):
+        return jnp.where(hit, 1.0, 0.0).astype(BF16)
+
+    def column(bias):
+        wide = jnp.broadcast_to(bias[...], (8, 8))
+        return jnp.sum(jnp.where(iota((8, 8), 0) == iota((8, 8), 1), wide, 0.0), axis=1, keepdims=True)
+
+    b1, b2 = column(raw_b1), column(raw_b2)
+    rows = jnp.concatenate([raw[k].astype(F32) for k in range(27)], axis=0)
+    wide2 = jnp.dot(
+        stacked(turned(rows[:, 0:8]), 3), one_hot(matches(216, 3, m1)), preferred_element_type=F32
+    )
+    tap = iota((16, 216), 1) >> 3
+    own_tap = one_hot(tap - 9 * third(tap, 9) == iota((16, 216), 0))
+    wide3 = jnp.dot(
+        own_tap,
+        jnp.where(matches(216, 3, m2), rows[:, 8:9], 0.0).astype(BF16),
+        preferred_element_type=F32,
+    )
+    tap = iota((72, 216), 1) >> 3
+    own_row = (tap - 9 * third(tap, 9)) * 8 + (iota((72, 216), 1) & 7) == iota((72, 216), 0)
+    same_a = third(iota((216, 6 * ny), 0) >> 3, 9) == third(iota((216, 6 * ny), 1), 2 * ny)
+    wide1 = jnp.dot(
+        one_hot(own_row),
+        jnp.where(same_a, rows[:, 9:10], 0.0).astype(BF16),
+        preferred_element_type=F32,
+    )
+    s1 = [wide1[8 * k : 8 * k + 8] for k in range(9)]
+    s2 = [wide2[8 * k : 8 * k + 8] for k in range(9)]
+    s3 = [wide3[k : k + 1] for k in range(9)]
     for e in range(3):
         band(w1, s1, e, r1, 8, -2, 2 * ny, grad_slot)
-        band(w2, s2_slabs, e, r2, 8, -1, r1 * 8, lambda s: (s >> 3) - 2)
+        band(w2, s2, e, r2, 8, -1, r1 * 8, lambda s: (s >> 3) - 2)
         band(w3, s3, e, ny, 1, 0, r2 * 8, lambda s: (s >> 3) - 1)
 
+    for load in loads[1:]:
+        load.wait()
+
+    def inner_one(x, carry):
+        center = ext_a[x + 4, 8 : 8 + ny, :]
+        out_next[x] = 2.0 * center - before[x] + speed[x] * laplace_z(center)
+        return carry
+
+    lax.fori_loop(0, nx, inner_one, 0, unroll=WAVE_UNROLL)
     for c in copies_a:
         c.arrive()
     unpack_wave(ext_a, recv_a)
 
     def step_one(x, carry):
-        center, lap = laplace_plane(ext_a, x, ny)
-        value = 2.0 * center - before[x] + speed[x] * lap
+        value = out_next[x] + speed[x] * laplace_xy(ext_a, x, ny)
         out_next[x] = value
         ext_b[x + 4, 8 : 8 + ny, :] = value
         return carry
@@ -242,13 +317,20 @@
     pack_wave(ext_b, pack_b)
     for c in copies_b:
         c.start()
+
+    def inner_two(x, carry):
+        center = out_next[x]
+        out_after[x] = 2.0 * center - ext_a[x + 4, 8 : 8 + ny, :] + speed[x] * laplace_z(center)
+        return carry
+
+    lax.fori_loop(0, nx, inner_two, 0, unroll=WAVE_UNROLL)
     for c in copies_b:
         c.arrive()
     unpack_wave(ext_b, recv_b)
 
     def step_two(x, carry):
-        center, lap = laplace_plane(ext_b, x, ny)
-        value = 2.0 * center - now[x] + speed[x] * lap
+        center = out_next[x]
+        value = out_after[x] + speed[x] * laplace_xy(ext_b, x, ny)
         out_after[x] = value
         gradient = prior[x] + src[0, x] * center + src[1, x] * value
         out_grad[x] = gradient
@@ -288,7 +370,7 @@
     def hidden(value, bias, rows, first, x):
         y = (lax.broadcasted_iota(jnp.int32, value.shape, 0) >> 3) + first
         inside = (y >= y_min) & (y < y_max) & (x >= x_min) & (x < x_max)
-        full = jnp.concatenate([jnp.broadcast_to(bias[...], (8, depth))] * rows, axis=0)
+        full = jnp.concatenate([jnp.broadcast_to(bias, (8, depth))] * rows, axis=0)
         return jnp.where(inside, jnp.maximum(value + full, 0.0), 0.0).astype(BF16)
 
     def layer_one(p, carry):
@@ -372,11 +454,9 @@
         c.wait_send()
 
 
-def slabs(weight, slots):
-    _, c, d = weight.shape
-    w = weight.astype(F32).reshape(3, 9, c, d).transpose(1, 3, 0, 2)
-    w = jnp.broadcast_to(w[:, :, :, None, :], (9, d, 3, slots, c))
-    return w.reshape(9, d, 3 * slots * c)
+def hand_on(*refs):
+    for source, target in zip(refs[:4], refs[4:]):
+        target[...] = source[...]
 
 
 def shards(n_gx, n_gy, speed, before, now, src, prior, w_first, b_first, w_mid, b_mid, w_last):
@@ -386,12 +466,17 @@
     half, groups = nx // 2, nx // 4
     r1, r2 = ny + 4, ny + 2
     ch = b_first.shape[0]
-    return pl.pallas_call(
+    outs = pl.pallas_call(
         functools.partial(kernel, n_gx, n_gy),
         out_shape=(out,) * 4,
-        in_specs=[vmem] * 10,
+        in_specs=[pl.BlockSpec(memory_space=pl.ANY)] * 5 + [vmem] * 3,
         out_specs=(vmem,) * 4,
         scratch_shapes=[
+            pltpu.VMEM(now.shape, F32),
+            pltpu.VMEM(now.shape, F32),
+            pltpu.VMEM(src.shape, F32),
+            pltpu.VMEM(now.shape, F32),
+            pltpu.SemaphoreType.DMA((5,)),
             pltpu.VMEM((nx + 8, ny + 16, depth), F32),
             pltpu.VMEM((nx + 8, ny + 16, depth), F32),
             pltpu.VMEM((2, half, 8, depth), F32),
@@ -417,7 +502,7 @@
             pltpu.SemaphoreType.DMA((n_gx,)),
         ],
         compiler_params=pltpu.CompilerParams(
-            collective_id=0, has_side_effects=True, vmem_limit_bytes=40 * 1024 * 1024
+            collective_id=0, has_side_effects=True, vmem_limit_bytes=60 * 1024 * 1024
         ),
     )(
         speed,
@@ -425,12 +510,18 @@
         now,
         src,
         prior,
-        slabs(w_first, 2 * ny),
-        w_mid.reshape(3, 9, ch, ch).transpose(1, 3, 0, 2).reshape(9 * ch, 3 * ch),
-        slabs(w_last, r2),
-        b_first.reshape(ch, 1),
-        b_mid.reshape(ch, 1),
+        jnp.concatenate([w_mid, w_last, w_first.reshape(27, ch, 1)], axis=2),
+        b_first.reshape(1, ch),
+        b_mid.reshape(1, ch),
     )
+    block = pl.BlockSpec((nx // 4, ny, depth), lambda i: (i, 0, 0))
+    return pl.pallas_call(
+        hand_on,
+        grid=(4,),
+        out_shape=(out,) * 4,
+        in_specs=[block] * 4,
+        out_specs=(block,) * 4,
+    )(*outs)
 
 
 def solution(mesh):

time: 39.4 us -> 37.4 us (0.949)
  local copies, waits for them, and re-layouts: 9.13 us -> 2.23 us
  Pallas kernels: 29.2 us -> 33.3 us
  other arithmetic: 0 us -> 0.73 us
    unnamed x24 -> x8, local copies, waits for them, and re-layouts: 7.64 us -> 2.07 us
    pallas_call x0 -> x1, Pallas kernels: none -> 3.34 us  [shards(): pl.pallas_call(hand_on, grid=(4,), out_shape=(out,) * 4, in_specs=[block]...]
    broadcast_in_dim x8 -> x0, local copies, waits for them, and re-layouts: 0.83 us -> none  [slabs(): w = jnp.broadcast_to(w[:, :, :, None, :], (9, d, 3, slots, c))]
    pallas_call x1, Pallas kernels: 29.2 us -> 30 us  [shards(): pl.pallas_call(functools.partial(kernel, n_gx, n_gy), out_shape=(out,) *...]
    concatenate x0 -> x1, other arithmetic: none -> 0.73 us  [shards(): jnp.concatenate([w_mid, w_last, w_first.reshape(27, ch, 1)], axis=2)]
where the time goes in v2:
time: 37.4 us; the launch traced here: 36.9 us
  Pallas kernels  33.3 us (89%)
  local copies, waits for them, and re-layouts  2.23 us (6%)
  other arithmetic  0.73 us (2%)
  between operations  0.65 us (2%)
    pallas_call x1, Pallas kernels, shards(): pl.pallas_call(functools.partial(kernel, n_gx, n_gy), out_shape=(out,) *...  30 us
    pallas_call x1, Pallas kernels, shards(): pl.pallas_call(hand_on, grid=(4,), out_shape=(out,) * 4, in_specs=[block]...  3.34 us
    unnamed x8, local copies, waits for them, and re-layouts  2.07 us

profile of v2, /device:TPU:0, one launch (start us, length us, event | category | flops | bytes accessed | tf_op | source)
XLA Modules:
  0.0 36.9 jit_solution(7922105439732887209)
XLA Ops:
  0.6 0.0 copy-start.1
  0.6 0.7 %copy-done.1 = bf16[27,1,8]{0,2,1:T(8,128)(2,1)S(1)} copy-done((bf16[27,1,8]{0,2,1:T(8,128)(2,1)S(1)}, bf16[27,1,8]{0,2,1:T(8,128)(2,1)}, u32[]{:S(2)}) %copy-start.1) | copy-done | bytes 456
  1.3 0.0 copy-start
  1.3 0.2 copy.24
  1.5 0.6 %copy-done = bf16[27,8,8]{0,2,1:T(8,128)(2,1)S(1)} copy-done((bf16[27,8,8]{0,2,1:T(8,128)(2,1)S(1)}, bf16[27,8,8]{0,2,1:T(8,128)(2,1)}, u32[]{:S(2)}) %copy-start) | copy-done | bytes 3480
  2.0 0.0 copy-start.2
  2.0 0.1 copy.22
  2.2 0.5 %copy-done.2 = bf16[27,8,1]{0,1,2:T(8,128)(2,1)S(1)} copy-done((bf16[27,8,1]{0,1,2:T(8,128)(2,1)S(1)}, bf16[27,8,1]{0,1,2:T(8,128)(2,1)}, u32[]{:S(2)}) %copy-start.2) | copy-done | bytes 456
  2.7 0.2 copy.23
  2.9 0.7 %pad_maximum_fusion.raw = bf16[27,8,10]{2,1,0:T(8,128)(2,1)} fusion(bf16[27,8,1]{2,1,0:T(8,128)(2,1)S(1)} %copy.24, bf16[27,8,1]{2,1,0:T(8,128)(2,1)S(1)} %copy.23, bf16[27,8,8]{2,1,0:T(8,128)(2,1)S(1)} %copy.22), kind=kLoop, calls=%fused_computation | loop fusion | flops 12960 | bytes 8640 | tf_op jit(solution)/shard_map/concatenate | solution.py:513
  3.6 30.0 %shard_map.129 = (f32[16,16,256]{2,1,0:T(8,128)}, f32[16,16,256]{2,1,0:T(8,128)}, f32[16,16,256]{2,1,0:T(8,128)}, f32[16,16,256]{2,1,0:T(8,128)}) custom-call(f32[16,16,256]{2,1,0:T(8,128)} %speed_hbm.1, f32[16,16,256]{2,1,0:T(8,128)} %before_hbm.1, f32[16,16,256]{2,1,0:T(8,128)} %now_hbm.1, f32[2,16,16,256]{3,2,1,0:T(8,128)} %src_hbm.1, ...), custom_call_target="tpu_custom_call" | custom-call | tf_op jit(solution)/shard_map/pallas_call | solution.py:469
  33.6 3.3 %shard_map.130 = (f32[16,16,256]{2,1,0:T(8,128)}, f32[16,16,256]{2,1,0:T(8,128)}, f32[16,16,256]{2,1,0:T(8,128)}, f32[16,16,256]{2,1,0:T(8,128)}) custom-call(f32[16,16,256]{2,1,0:T(8,128)} %get-tuple-element.8.refs_0_, f32[16,16,256]{2,1,0:T(8,128)} %get-tuple-element.9.refs_1_, f32[16,16,256]{2,1,0:T(8,128)} %get-tuple-element.10.refs_2_, ...), custom_call_target="tpu_custom_call" | custom-call | tf_op jit(solution)/shard_map/pallas_call | solution.py:518
Async XLA Ops:
  0.6 0.7 %copy-start.1 = (bf16[27,1,8]{0,2,1:T(8,128)(2,1)S(1)}, bf16[27,1,8]{0,2,1:T(8,128)(2,1)}, u32[]{:S(2)}) copy-start(bf16[27,1,8]{0,2,1:T(8,128)(2,1)} %param.15) | copy-start | bytes 1300
  1.3 0.7 %copy-start = (bf16[27,8,8]{0,2,1:T(8,128)(2,1)S(1)}, bf16[27,8,8]{0,2,1:T(8,128)(2,1)}, u32[]{:S(2)}) copy-start(bf16[27,8,8]{0,2,1:T(8,128)(2,1)} %param.17) | copy-start | bytes 10372
  2.0 0.7 %copy-start.2 = (bf16[27,8,1]{0,1,2:T(8,128)(2,1)S(1)}, bf16[27,8,1]{0,1,2:T(8,128)(2,1)}, u32[]{:S(2)}) copy-start(bf16[27,8,1]{0,1,2:T(8,128)(2,1)} %param.19) | copy-start | bytes 1300

commit v3 on v2

--- a/solution.py
+++ b/solution.py
@@ -12,7 +12,7 @@
 F32 = jnp.float32
 BF16 = jnp.bfloat16
 UNROLL = True
-WAVE_UNROLL = 4
+WAVE_UNROLL = 8
 
 
 def shift_z(v, k):
@@ -314,8 +314,10 @@
         return carry
 
     lax.fori_loop(0, nx, step_one, 0, unroll=WAVE_UNROLL)
+    for c in copies_b[:2]:
+        c.start()
     pack_wave(ext_b, pack_b)
-    for c in copies_b:
+    for c in copies_b[2:]:
         c.start()
 
     def inner_two(x, carry):
@@ -338,12 +340,14 @@
         return carry
 
     lax.fori_loop(0, nx, step_two, 0, unroll=WAVE_UNROLL)
+    for c in copies_g[:2]:
+        c.start()
     for t in range(groups):
         for side, at in ((0, 0), (1, ny - 4)):
             pack_g[side, t] = jnp.concatenate(
                 [out_grad[4 * t + j, at : at + 4, :] for j in range(4)], axis=0
             ).astype(BF16)
-    for c in copies_g:
+    for c in copies_g[2:]:
         c.start()
     for c in copies_g:
         c.arrive()

time: 37.4 us -> 37.4 us (level)
  no operation moved by 1% of the time
where the time goes in v3:
time: 37.4 us; the launch traced here: 36.9 us
  Pallas kernels  33.3 us (89%)
  local copies, waits for them, and re-layouts  2.23 us (6%)
  other arithmetic  0.73 us (2%)
  between operations  0.65 us (2%)
    pallas_call x1, Pallas kernels, shards(): pl.pallas_call(functools.partial(kernel, n_gx, n_gy), out_shape=(out,) *...  29.9 us
    pallas_call x1, Pallas kernels, shards(): pl.pallas_call(hand_on, grid=(4,), out_shape=(out,) * 4, in_specs=[block]...  3.34 us
    unnamed x8, local copies, waits for them, and re-layouts  2.07 us

profile of v3, /device:TPU:0, one launch (start us, length us, event | category | flops | bytes accessed | tf_op | source)
XLA Modules:
  0.0 36.9 jit_solution(17061647696929609338)
XLA Ops:
  0.6 0.0 copy-start.1
  0.6 0.7 %copy-done.1 = bf16[27,1,8]{0,2,1:T(8,128)(2,1)S(1)} copy-done((bf16[27,1,8]{0,2,1:T(8,128)(2,1)S(1)}, bf16[27,1,8]{0,2,1:T(8,128)(2,1)}, u32[]{:S(2)}) %copy-start.1) | copy-done | bytes 456
  1.3 0.0 copy-start
  1.3 0.2 copy.24
  1.5 0.6 %copy-done = bf16[27,8,8]{0,2,1:T(8,128)(2,1)S(1)} copy-done((bf16[27,8,8]{0,2,1:T(8,128)(2,1)S(1)}, bf16[27,8,8]{0,2,1:T(8,128)(2,1)}, u32[]{:S(2)}) %copy-start) | copy-done | bytes 3480
  2.0 0.0 copy-start.2
  2.0 0.1 copy.22
  2.2 0.5 %copy-done.2 = bf16[27,8,1]{0,1,2:T(8,128)(2,1)S(1)} copy-done((bf16[27,8,1]{0,1,2:T(8,128)(2,1)S(1)}, bf16[27,8,1]{0,1,2:T(8,128)(2,1)}, u32[]{:S(2)}) %copy-start.2) | copy-done | bytes 456
  2.7 0.2 copy.23
  2.9 0.7 %pad_maximum_fusion.raw = bf16[27,8,10]{2,1,0:T(8,128)(2,1)} fusion(bf16[27,8,1]{2,1,0:T(8,128)(2,1)S(1)} %copy.24, bf16[27,8,1]{2,1,0:T(8,128)(2,1)S(1)} %copy.23, bf16[27,8,8]{2,1,0:T(8,128)(2,1)S(1)} %copy.22), kind=kLoop, calls=%fused_computation | loop fusion | flops 12960 | bytes 8640 | tf_op jit(solution)/shard_map/concatenate | solution.py:517
  3.6 29.9 %shard_map.129 = (f32[16,16,256]{2,1,0:T(8,128)}, f32[16,16,256]{2,1,0:T(8,128)}, f32[16,16,256]{2,1,0:T(8,128)}, f32[16,16,256]{2,1,0:T(8,128)}) custom-call(f32[16,16,256]{2,1,0:T(8,128)} %speed_hbm.1, f32[16,16,256]{2,1,0:T(8,128)} %before_hbm.1, f32[16,16,256]{2,1,0:T(8,128)} %now_hbm.1, f32[2,16,16,256]{3,2,1,0:T(8,128)} %src_hbm.1, ...), custom_call_target="tpu_custom_call" | custom-call | tf_op jit(solution)/shard_map/pallas_call | solution.py:473
  33.6 3.3 %shard_map.130 = (f32[16,16,256]{2,1,0:T(8,128)}, f32[16,16,256]{2,1,0:T(8,128)}, f32[16,16,256]{2,1,0:T(8,128)}, f32[16,16,256]{2,1,0:T(8,128)}) custom-call(f32[16,16,256]{2,1,0:T(8,128)} %get-tuple-element.8.refs_0_, f32[16,16,256]{2,1,0:T(8,128)} %get-tuple-element.9.refs_1_, f32[16,16,256]{2,1,0:T(8,128)} %get-tuple-element.10.refs_2_, ...), custom_call_target="tpu_custom_call" | custom-call | tf_op jit(solution)/shard_map/pallas_call | solution.py:522
Async XLA Ops:
  0.6 0.7 %copy-start.1 = (bf16[27,1,8]{0,2,1:T(8,128)(2,1)S(1)}, bf16[27,1,8]{0,2,1:T(8,128)(2,1)}, u32[]{:S(2)}) copy-start(bf16[27,1,8]{0,2,1:T(8,128)(2,1)} %param.15) | copy-start | bytes 1300
  1.3 0.7 %copy-start = (bf16[27,8,8]{0,2,1:T(8,128)(2,1)S(1)}, bf16[27,8,8]{0,2,1:T(8,128)(2,1)}, u32[]{:S(2)}) copy-start(bf16[27,8,8]{0,2,1:T(8,128)(2,1)} %param.17) | copy-start | bytes 10372
  2.0 0.7 %copy-start.2 = (bf16[27,8,1]{0,1,2:T(8,128)(2,1)S(1)}, bf16[27,8,1]{0,1,2:T(8,128)(2,1)}, u32[]{:S(2)}) copy-start(bf16[27,8,1]{0,1,2:T(8,128)(2,1)} %param.19) | copy-start | bytes 1300
